TPU v7x, 32 devices: a whole 2x2x4 slice. The times are simulated.
32 devices in a mesh: group: 2 (over y), gx: 4 (over z), gy: 2 (over x), gz: 2 (over core).
Axes of the slice: x: 2, y: 2, z: 4, core: 2. Of those that a mesh axis runs over, the one named last changes fastest.
Arguments:
- board_temp: float32 [32, 256, 1024], P('group', 'gx', ('gy', 'gz')), parts along dimension 0, may hold values from -4 to 4
- board_coeff: float32 [32, 256, 1024], P('group', 'gx', ('gy', 'gz')), parts along dimension 0, may hold values from 0.03 to 0.12
- source: float32 [512, 1024], P(('group', 'gx'), ('gy', 'gz')), parts along dimension 0, may hold values from -4 to 4
- board_target: float32 [32, 256, 1024], P('group', 'gx', ('gy', 'gz')), parts along dimension 0, may hold values from -4 to 4
- pipe_temp: float32 [896, 2048], P(('group', 'gy', 'gz'), 'gx'), parts along dimension 0, may hold values from -4 to 4
- pipe_target: float32 [896, 2048], P(('group', 'gy', 'gz'), 'gx'), parts along dimension 0, may hold values from -4 to 4
- pipe_cond: float32 [896], P(('group', 'gy', 'gz')), parts along dimension 0, may hold values from 0.1 to 0.45
- contact_gain: float32 [896], P(('group', 'gy', 'gz')), parts along dimension 0, may hold values from 0.1 to 0.4
- contact_col: int32 [896, 2048], P(('group', 'gy', 'gz'), 'gx'), parts along dimension 0, may hold values from 0 to 255
- pipe_owner: int32 [896], P(('group', 'gy', 'gz')), parts along dimension 0, may hold values from 0 to 3, as said below
- step_index: int32 [2], P('group'), parts along dimension 0, may hold values from 0 to 99999
Outputs:
- board_adjoint: float32 [32, 256, 1024], P('group', 'gx', ('gy', 'gz')), parts along dimension 0
- pipe_adjoint: float32 [896, 2048], P(('group', 'gy', 'gz'), 'gx'), parts along dimension 0
- source_gradient: float32 [512, 1024], P(('group', 'gx'), ('gy', 'gz')), parts along dimension 0
There are 2 independent parts, one for each index of `group`. A program takes and returns all parts, laid end to end along the dimension named above; each array names one. Nothing has to cross between parts.
Inputs may be any that keep to these rules, and one draw needn't show every extreme that they name: `pipe_owner`: in each aligned block of 112 pipes one strip, the same in every block, has exactly 28 of the block's pipes, and no strip has more than 28 of them.
All inputs are finite; a program needn't handle non-finite values.
Results may differ from a plain program's by a relative error of at most 0.0003.
Values sent between devices are 32-bit elements; how exact they have to be, the bound alone decides.
A program may use at most 64 MiB of HBM per device.

v0:
```python
import math

import jax
import jax.numpy as jnp
from jax import lax
from jax.sharding import PartitionSpec as P

CUBIC_TERM = 0.05
BOARD_SHARE = 0.5
PIPE_SHARE = 1.0
VERTICAL = 1.0
PERIOD_STEPS = 24.0
EXACT = lax.Precision.HIGHEST


def extended(block, sides, width):
    for axis, dim in sides:
        count = lax.axis_size(axis)
        forward = [(i, i + 1) for i in range(count - 1)]
        backward = [(target, source) for source, target in forward]
        low = lax.ppermute(
            lax.slice_in_dim(block, block.shape[dim] - width, None, axis=dim), axis, forward
        )
        high = lax.ppermute(lax.slice_in_dim(block, 0, width, axis=dim), axis, backward)
        block = jnp.concatenate([low, block, high], axis=dim)
    return block


def power(moment):
    return 1.0 + 0.5 * jnp.sin(2.0 * math.pi / PERIOD_STEPS * moment.astype(jnp.float32))


def lap_board(field):
    padded = extended(field, (("gx", 1), (("gy", "gz"), 2)), 1)
    lateral = (
        padded[:, 2:, 1:-1]
        + padded[:, :-2, 1:-1]
        + padded[:, 1:-1, 2:]
        + padded[:, 1:-1, :-2]
        - 4.0 * field
    )
    deeper = jnp.pad(field, ((1, 1), (0, 0), (0, 0)))
    across = deeper[2:] + deeper[:-2] - 2.0 * field
    return lateral + VERTICAL * across


def local(
    board_temp,
    board_coeff,
    source,
    board_target,
    pipe_temp,
    pipe_target,
    pipe_cond,
    contact_gain,
    contact_col,
    pipe_owner,
    step_index,
):
    tile_rows = board_temp.shape[1]
    tile_cols = board_temp.shape[2]
    pipe_count, node_count = pipe_temp.shape
    owners = lax.axis_size(("gy", "gz"))
    segment = lax.axis_index("gx")
    total_nodes = node_count * lax.axis_size("gx")
    local_node = jnp.arange(node_count, dtype=jnp.int32)
    node_rows = local_node * tile_rows // node_count
    row_hot = (node_rows[:, None] == jnp.arange(tile_rows, dtype=jnp.int32)[None, :]).astype(
        jnp.float32
    )
    col_range = jnp.arange(tile_cols, dtype=jnp.int32)
    global_node = segment * node_count + local_node
    right_ok = global_node < total_nodes - 1
    left_ok = global_node > 0
    gain = contact_gain[:, None]
    conduct = pipe_cond[:, None]

    def node_values(board_top):
        return jnp.dot(row_hot, board_top, precision=EXACT, preferred_element_type=jnp.float32)

    def rows_of_nodes(per_node):
        return jnp.dot(row_hot.T, per_node, precision=EXACT, preferred_element_type=jnp.float32)

    def lap_chain(field):
        padded = extended(field, (("gx", 1),), 1)
        right = jnp.where(right_ok, padded[:, 2:] - field, 0.0)
        left = jnp.where(left_ok, padded[:, :-2] - field, 0.0)
        return right + left

    owner_hot = (pipe_owner[:, None] == jnp.arange(owners, dtype=jnp.int32)[None, :]).astype(
        jnp.float32
    )
    col_mask = contact_col[:, :, None] == col_range[None, None, :]

    def fetch_strip(board_top):
        strip = lax.all_gather(board_top, ("gy", "gz"), axis=1, tiled=True)
        values = node_values(strip).reshape(node_count, owners, tile_cols)
        pipe_rows = jnp.einsum("po,joc->pjc", owner_hot, values, precision=EXACT)
        return jnp.sum(jnp.where(col_mask, pipe_rows, 0.0), axis=2)

    def spread_back(values):
        per_pipe = jnp.where(col_mask, values[:, :, None], 0.0)
        wide = jnp.einsum("po,pjc->joc", owner_hot, per_pipe, precision=EXACT)
        wide = rows_of_nodes(wide.reshape(node_count, owners * tile_cols))
        return lax.psum_scatter(wide, ("gy", "gz"), scatter_dimension=1, tiled=True)

    def couple(board_top, pipes):
        differ = pipes - fetch_strip(board_top)
        flux = gain * (differ + CUBIC_TERM * differ * differ * differ)
        weight = gain * (1.0 + 3.0 * CUBIC_TERM * differ * differ)
        return (spread_back(flux), flux, weight)

    def couple_back(adjoint_top, pipe_adj, weight):
        sensed = (BOARD_SHARE * fetch_strip(adjoint_top) - PIPE_SHARE * pipe_adj) * weight
        return (spread_back(sensed), sensed)

    def forward(board, pipes, moment):
        deposit, flux, weight = couple(board[0], pipes)
        board_next = board + board_coeff * lap_board(board)
        upper = board_next[0] + power(moment) * source + BOARD_SHARE * deposit
        board_next = board_next.at[0].set(upper)
        pipe_next = pipes + conduct * lap_chain(pipes) - PIPE_SHARE * flux
        return (board_next, pipe_next, weight)

    def backward(board_adj, pipe_adj, weight):
        deposit, sensed = couple_back(board_adj[0], pipe_adj, weight)
        board_prev = board_adj + lap_board(board_coeff * board_adj)
        board_prev = board_prev.at[0].add(-deposit)
        pipe_prev = pipe_adj + conduct * lap_chain(pipe_adj) + sensed
        return (board_prev, pipe_prev)

    start = step_index[0]
    board_one, pipe_one, weight_zero = forward(board_temp, pipe_temp, start)
    board_two, pipe_two, weight_one = forward(board_one, pipe_one, start + 1)
    seed_board = board_two - board_target
    seed_pipe = pipe_two - pipe_target
    adj_board_one, adj_pipe_one = backward(seed_board, seed_pipe, weight_one)
    board_adjoint, pipe_adjoint = backward(adj_board_one, adj_pipe_one, weight_zero)
    source_gradient = power(start + 1) * seed_board[0] + power(start) * adj_board_one[0]
    return (board_adjoint, pipe_adjoint, source_gradient)


def solution(mesh):
    placed = (
        P("group", "gx", ("gy", "gz")),
        P("group", "gx", ("gy", "gz")),
        P(("group", "gx"), ("gy", "gz")),
        P("group", "gx", ("gy", "gz")),
        P(("group", "gy", "gz"), "gx"),
        P(("group", "gy", "gz"), "gx"),
        P(("group", "gy", "gz")),
        P(("group", "gy", "gz")),
        P(("group", "gy", "gz"), "gx"),
        P(("group", "gy", "gz")),
        P("group"),
    )
    return jax.shard_map(
        local,
        mesh=mesh,
        in_specs=placed,
        out_specs=(
            P("group", "gx", ("gy", "gz")),
            P(("group", "gy", "gz"), "gx"),
            P(("group", "gx"), ("gy", "gz")),
        ),
        check_vma=False,
    )
```

profile of v0, /device:TPU:1, one launch (start us, length us, event | category | flops | bytes accessed | tf_op | source)
XLA Modules:
  0.0 519.6 jit_solution(14893049183241434763)
XLA Ops:
  9.6 4.7 collective-permute-start.9
  16.6 4.0 collective-permute-start.1
  21.4 7.5 %all-gather = f32[1,64,1024]{2,1,0:T(8,128)S(1)} all-gather(f32[1,64,256]{2,1,0:T(8,128)S(1)} %slice.305), channel_id=2, replica_groups=mesh['group'=2,'gx'=4,'gy'=2,'gz'=2] {'gy','gz'}, dimensions={2}, use_global_device_ids=true | all-gather | bytes 327680 | tf_op jit(solution)/shard_map/all_gather | solution.py:96
  33.8 45.4 %select_reduce_fusion.3 = f32[112,512]{0,1:T(8,128)S(1)} fusion(s32[112,512]{0,1:T(8,128)S(1)} %copy.23, f32[512,4,256]{2,1,0:T(4,128)} %reshape.188, s32[112]{0:T(128)S(1)} %copy-done.27), kind=kOutput, calls=%fused_computation.11 | convolution fusion | flops 748626368 | bytes 2556352 | tf_op jit(solution)/shard_map/po,joc->pjc/dot_general | solution.py:98
  79.6 37.2 %fusion.6 = f32[512,256,4]{1,2,0:T(4,128)S(1)} fusion(f32[112,512]{0,1:T(8,128)S(1)} %get-tuple-element.65, s32[112,512]{0,1:T(8,128)S(1)} %copy.23, s32[112]{0:T(128)S(1)} %copy-done.27), kind=kOutput, calls=%fused_computation.9 | convolution fusion | flops 734003648 | bytes 2556352 | tf_op jit(solution)/shard_map/po,pjc->joc/dot_general | solution.py:103
  123.9 3.5 collective-permute-start.3
  128.7 4.0 collective-permute-start.15
  139.8 6.4 %all_gather.13 = f32[64,1024]{1,0:T(8,128)S(1)} all-gather(f32[64,256]{1,0:T(8,128)S(1)} %fusion.120), channel_id=1, replica_groups=mesh['group'=2,'gx'=4,'gy'=2,'gz'=2] {'gy','gz'}, dimensions={1}, use_global_device_ids=true | all-gather | bytes 327680 | tf_op jit(solution)/shard_map/all_gather | solution.py:96
  147.5 4.2 collective-permute-start.5
  154.0 3.2 reshape.190
  157.2 45.5 %select_reduce_fusion.2 = f32[112,512]{0,1:T(8,128)S(1)} fusion(s32[112,512]{0,1:T(8,128)S(1)} %copy-done.17, f32[512,4,256]{2,1,0:T(4,128)} %reshape.190, s32[112]{0:T(128)S(1)} %copy-done.27), kind=kOutput, calls=%fused_computation.8 | convolution fusion | flops 748626368 | bytes 2556352 | tf_op jit(solution)/shard_map/po,joc->pjc/dot_general | solution.py:98
  203.0 37.2 %fusion.4 = f32[512,256,4]{1,2,0:T(4,128)S(1)} fusion(f32[112,512]{0,1:T(8,128)S(1)} %get-tuple-element.61, s32[112,512]{0,1:T(8,128)S(1)} %copy-done.18, s32[112]{0:T(128)S(1)} %copy-done.27), kind=kOutput, calls=%fused_computation.6 | convolution fusion | flops 734003648 | bytes 2556352 | tf_op jit(solution)/shard_map/po,pjc->joc/dot_general | solution.py:103
  252.1 4.0 collective-permute-start.21
  264.9 6.5 %all-gather.1 = f32[1,64,1024]{2,1,0:T(8,128)S(1)} all-gather(f32[1,64,256]{2,1,0:T(8,128)S(1)} %slice.372), channel_id=3, replica_groups=mesh['group'=2,'gx'=4,'gy'=2,'gz'=2] {'gy','gz'}, dimensions={2}, use_global_device_ids=true | all-gather | bytes 327680 | tf_op jit(solution)/shard_map/all_gather | solution.py:96
  277.1 45.5 %select_reduce_fusion.1 = f32[112,512]{0,1:T(8,128)S(1)} fusion(s32[112,512]{0,1:T(8,128)S(1)} %copy-done.19, f32[512,4,256]{2,1,0:T(4,128)} %reshape.193, s32[112]{0:T(128)S(1)} %copy-done.27), kind=kOutput, calls=%fused_computation.5 | convolution fusion | flops 748626368 | bytes 2556352 | tf_op jit(solution)/shard_map/po,joc->pjc/dot_general | solution.py:98
  322.9 37.2 %fusion.2 = f32[512,256,4]{1,2,0:T(4,128)S(1)} fusion(f32[112,512]{0,1:T(8,128)S(1)} %get-tuple-element.59, s32[112,512]{0,1:T(8,128)S(1)} %copy-done.20, s32[112]{0:T(128)S(1)} %copy-done.27), kind=kOutput, calls=%fused_computation.3 | convolution fusion | flops 734003648 | bytes 2556352 | tf_op jit(solution)/shard_map/po,pjc->joc/dot_general | solution.py:103
  361.9 4.0 collective-permute-start.11
  377.3 4.0 collective-permute-start.23
  388.4 6.6 %all-gather.2 = f32[1,64,1024]{2,1,0:T(8,128)S(1)} all-gather(f32[1,64,256]{2,1,0:T(8,128)S(1)} %get-tuple-element.55), channel_id=4, replica_groups=mesh['group'=2,'gx'=4,'gy'=2,'gz'=2] {'gy','gz'}, dimensions={2}, use_global_device_ids=true | all-gather | bytes 327680 | tf_op jit(solution)/shard_map/all_gather | solution.py:96
  397.4 3.2 reshape.196
  400.6 45.5 %select_reduce_fusion = f32[112,512]{0,1:T(8,128)S(1)} fusion(s32[112,512]{0,1:T(8,128)S(1)} %copy-done.21, f32[512,4,256]{2,1,0:T(4,128)} %reshape.196, s32[112]{0:T(128)S(1)} %copy-done.27), kind=kOutput, calls=%fused_computation.2 | convolution fusion | flops 748626368 | bytes 2556352 | tf_op jit(solution)/shard_map/po,joc->pjc/dot_general | solution.py:98
  447.1 37.1 %fusion = f32[512,256,4]{1,2,0:T(4,128)S(1)} fusion(f32[112,512]{0,1:T(8,128)S(1)} %get-tuple-element.57, s32[112,512]{0,1:T(8,128)S(1)} %copy-done.21, s32[112]{0:T(128)S(1)} %copy-done.27), kind=kOutput, calls=%fused_computation | convolution fusion | flops 734003648 | bytes 2556352 | tf_op jit(solution)/shard_map/po,pjc->joc/dot_general | solution.py:103
  486.2 4.0 collective-permute-start.17
  505.5 5.7 %reduce-scatter.11.cloned.1.call-done = f32[64,256]{1,0:T(8,128)} async-done(((f32[64,1024]{1,0:T(8,128)}), f32[64,256]{1,0:T(8,128)}) %reduce-scatter.11.cloned.1.call-update) | async-done | bytes 65552 | tf_op jit(solution)/shard_map/reduce_scatter | solution.py:105
  (176 shorter events, 97.7 us)
Async XLA Ops:
  7.2 131.7 %reduce-scatter.5.cloned.1.call-start = ((), (), s32[]{:S(2)}) async-start(), calls=%async_computation.4 | async-start | bytes 327680 | tf_op jit(solution)/shard_map/reduce_scatter | solution.py:105
  8.3 71.1 %collective-permute-start.8 = (f32[112,1]{0,1:T(1,128)S(1)}, f32[112,1]{0,1:T(1,128)S(1)}, u32[]{:S(2)}, u32[]{:S(2)}) collective-permute-start(f32[112,1]{0,1:T(1,128)S(1)} %get-tuple-element.88), channel_id=1, source_target_pairs={{4,0},{8,4},{12,8},{5,1},{9,5},{13,9},{6,2},{10,6},{14,10},{7,3},{... | collective-permute-start | bytes 1352 | tf_op jit(solution)/shard_map/ppermute | solution.py:24
  9.6 69.8 %collective-permute-start.9 = (f32[112,1]{0,1:T(1,128)S(1)}, f32[112,1]{0,1:T(1,128)S(1)}, u32[]{:S(2)}, u32[]{:S(2)}) collective-permute-start(f32[112,1]{0,1:T(1,128)S(1)} %get-tuple-element.89), channel_id=1, source_target_pairs={{0,4},{4,8},{8,12},{1,5},{5,9},{9,13},{2,6},{6,10},{10,14},{3,7},{... | collective-permute-start | bytes 1352 | tf_op jit(solution)/shard_map/ppermute | solution.py:21
  15.3 103.8 %collective-permute-start = (f32[16,1,256]{2,1,0:T(1,128)S(1)}, f32[16,1,256]{2,1,0:T(1,128)S(1)}, u32[]{:S(2)}, u32[]{:S(2)}) collective-permute-start(f32[16,1,256]{2,1,0:T(1,128)S(1)} %get-tuple-element.81), channel_id=1, source_target_pairs={{4,0},{8,4},{12,8},{5,1},{9,5},{13,9},{6,2},{10,6},{14,10},{7,3},{... | collective-permute-start | bytes 49160 | tf_op jit(solution)/shard_map/ppermute | solution.py:24
  16.6 102.5 %collective-permute-start.1 = (f32[16,1,256]{2,1,0:T(1,128)S(1)}, f32[16,1,256]{2,1,0:T(1,128)S(1)}, u32[]{:S(2)}, u32[]{:S(2)}) collective-permute-start(f32[16,1,256]{2,1,0:T(1,128)S(1)} %get-tuple-element.80), channel_id=1, source_target_pairs={{0,4},{4,8},{8,12},{1,5},{5,9},{9,13},{2,6},{6,10},{10,14},{3,7},{... | collective-permute-start | bytes 49160 | tf_op jit(solution)/shard_map/ppermute | solution.py:21
  119.0 142.7 %reduce-scatter.7.cloned.1.call-start = ((), (), s32[]{:S(2)}) async-start(), calls=%async_computation.5 | async-start | bytes 327680 | tf_op jit(solution)/shard_map/reduce_scatter | solution.py:105
  121.5 11.2 %collective-permute-start.2 = (f32[16,66,1]{1,0,2:T(8,128)S(1)}, f32[16,66,1]{1,0,2:T(8,128)S(1)}, u32[]{:S(2)}, u32[]{:S(2)}) collective-permute-start(f32[16,66,1]{1,0,2:T(8,128)S(1)} %copy.19), channel_id=1, source_target_pairs={{1,0},{2,1},{3,2},{5,4},{6,5},{7,6},{9,8},{10,9},{11,10},{13,12},{... | collective-permute-start | bytes 12680 | tf_op jit(solution)/shard_map/ppermute | solution.py:24
  123.9 10.0 %collective-permute-start.3 = (f32[16,66,1]{1,0,2:T(8,128)S(1)}, f32[16,66,1]{1,0,2:T(8,128)S(1)}, u32[]{:S(2)}, u32[]{:S(2)}) collective-permute-start(f32[16,66,1]{1,0,2:T(8,128)S(1)} %copy.21), channel_id=1, source_target_pairs={{0,1},{1,2},{2,3},{4,5},{5,6},{6,7},{8,9},{9,10},{10,11},{12,13},{... | collective-permute-start | bytes 12680 | tf_op jit(solution)/shard_map/ppermute | solution.py:21
  127.4 75.4 %collective-permute-start.14 = (f32[112,1]{0,1:T(1,128)S(1)}, f32[112,1]{0,1:T(1,128)S(1)}, u32[]{:S(2)}, u32[]{:S(2)}) collective-permute-start(f32[112,1]{0,1:T(1,128)S(1)} %get-tuple-element.86), channel_id=1, source_target_pairs={{4,0},{8,4},{12,8},{5,1},{9,5},{13,9},{6,2},{10,6},{14,10},{7,3},{... | collective-permute-start | bytes 1352 | tf_op jit(solution)/shard_map/ppermute | solution.py:24
  128.7 74.1 %collective-permute-start.15 = (f32[112,1]{0,1:T(1,128)S(1)}, f32[112,1]{0,1:T(1,128)S(1)}, u32[]{:S(2)}, u32[]{:S(2)}) collective-permute-start(f32[112,1]{0,1:T(1,128)S(1)} %get-tuple-element.87), channel_id=1, source_target_pairs={{0,4},{4,8},{8,12},{1,5},{5,9},{9,13},{2,6},{6,10},{10,14},{3,7},{... | collective-permute-start | bytes 1352 | tf_op jit(solution)/shard_map/ppermute | solution.py:21
  146.2 96.3 %collective-permute-start.4 = (f32[16,1,256]{2,1,0:T(1,128)S(1)}, f32[16,1,256]{2,1,0:T(1,128)S(1)}, u32[]{:S(2)}, u32[]{:S(2)}) collective-permute-start(f32[16,1,256]{2,1,0:T(1,128)S(1)} %get-tuple-element.79), channel_id=1, source_target_pairs={{4,0},{8,4},{12,8},{5,1},{9,5},{13,9},{6,2},{10,6},{14,10},{7,3},{... | collective-permute-start | bytes 49160 | tf_op jit(solution)/shard_map/ppermute | solution.py:24
  147.5 95.0 %collective-permute-start.5 = (f32[16,1,256]{2,1,0:T(1,128)S(1)}, f32[16,1,256]{2,1,0:T(1,128)S(1)}, u32[]{:S(2)}, u32[]{:S(2)}) collective-permute-start(f32[16,1,256]{2,1,0:T(1,128)S(1)} %get-tuple-element.78), channel_id=1, source_target_pairs={{0,4},{4,8},{8,12},{1,5},{5,9},{9,13},{2,6},{6,10},{10,14},{3,7},{... | collective-permute-start | bytes 49160 | tf_op jit(solution)/shard_map/ppermute | solution.py:21
  242.4 144.4 %reduce-scatter.9.cloned.1.call-start = ((), (), s32[]{:S(2)}) async-start(), calls=%async_computation.6 | async-start | bytes 327680 | tf_op jit(solution)/shard_map/reduce_scatter | solution.py:105
  244.9 11.2 %collective-permute-start.6 = (f32[16,66,1]{1,0,2:T(8,128)S(1)}, f32[16,66,1]{1,0,2:T(8,128)S(1)}, u32[]{:S(2)}, u32[]{:S(2)}) collective-permute-start(f32[16,66,1]{1,0,2:T(8,128)S(1)} %copy.25), channel_id=1, source_target_pairs={{1,0},{2,1},{3,2},{5,4},{6,5},{7,6},{9,8},{10,9},{11,10},{13,12},{... | collective-permute-start | bytes 12680 | tf_op jit(solution)/shard_map/ppermute | solution.py:24
  247.8 9.4 %collective-permute-start.7 = (f32[16,66,1]{1,0,2:T(8,128)S(1)}, f32[16,66,1]{1,0,2:T(8,128)S(1)}, u32[]{:S(2)}, u32[]{:S(2)}) collective-permute-start(f32[16,66,1]{1,0,2:T(8,128)S(1)} %copy.27), channel_id=1, source_target_pairs={{0,1},{1,2},{2,3},{4,5},{5,6},{6,7},{8,9},{9,10},{10,11},{12,13},{... | collective-permute-start | bytes 12680 | tf_op jit(solution)/shard_map/ppermute | solution.py:21
  250.8 71.8 %collective-permute-start.20 = (f32[112,1]{0,1:T(1,128)S(1)}, f32[112,1]{0,1:T(1,128)S(1)}, u32[]{:S(2)}, u32[]{:S(2)}) collective-permute-start(f32[112,1]{0,1:T(1,128)S(1)} %get-tuple-element.84), channel_id=1, source_target_pairs={{4,0},{8,4},{12,8},{5,1},{9,5},{13,9},{6,2},{10,6},{14,10},{7,3},{... | collective-permute-start | bytes 1352 | tf_op jit(solution)/shard_map/ppermute | solution.py:24
  252.1 70.6 %collective-permute-start.21 = (f32[112,1]{0,1:T(1,128)S(1)}, f32[112,1]{0,1:T(1,128)S(1)}, u32[]{:S(2)}, u32[]{:S(2)}) collective-permute-start(f32[112,1]{0,1:T(1,128)S(1)} %get-tuple-element.85), channel_id=1, source_target_pairs={{0,4},{4,8},{8,12},{1,5},{5,9},{9,13},{2,6},{6,10},{10,14},{3,7},{... | collective-permute-start | bytes 1352 | tf_op jit(solution)/shard_map/ppermute | solution.py:21
  360.6 7.1 %collective-permute-start.10 = (f32[16,1,256]{2,1,0:T(1,128)S(1)}, f32[16,1,256]{2,1,0:T(1,128)S(1)}, u32[]{:S(2)}, u32[]{:S(2)}) collective-permute-start(f32[16,1,256]{2,1,0:T(1,128)S(1)} %get-tuple-element.77), channel_id=1, source_target_pairs={{4,0},{8,4},{12,8},{5,1},{9,5},{13,9},{6,2},{10,6},{14,10},{7,3},{... | collective-permute-start | bytes 49160 | tf_op jit(solution)/shard_map/ppermute | solution.py:24
  367.6 143.5 %reduce-scatter.11.cloned.1.call-start = ((), (), s32[]{:S(2)}) async-start(), calls=%async_computation.7 | async-start | bytes 327680 | tf_op jit(solution)/shard_map/reduce_scatter | solution.py:105
  370.1 11.2 %collective-permute-start.12 = (f32[16,66,1]{1,0,2:T(8,128)S(1)}, f32[16,66,1]{1,0,2:T(8,128)S(1)}, u32[]{:S(2)}, u32[]{:S(2)}) collective-permute-start(f32[16,66,1]{1,0,2:T(8,128)S(1)} %copy.36), channel_id=1, source_target_pairs={{1,0},{2,1},{3,2},{5,4},{6,5},{7,6},{9,8},{10,9},{11,10},{13,12},{... | collective-permute-start | bytes 12680 | tf_op jit(solution)/shard_map/ppermute | solution.py:24
  373.0 9.4 %collective-permute-start.13 = (f32[16,66,1]{1,0,2:T(8,128)S(1)}, f32[16,66,1]{1,0,2:T(8,128)S(1)}, u32[]{:S(2)}, u32[]{:S(2)}) collective-permute-start(f32[16,66,1]{1,0,2:T(8,128)S(1)} %copy.38), channel_id=1, source_target_pairs={{0,1},{1,2},{2,3},{4,5},{5,6},{6,7},{8,9},{9,10},{10,11},{12,13},{... | collective-permute-start | bytes 12680 | tf_op jit(solution)/shard_map/ppermute | solution.py:21
  376.0 70.1 %collective-permute-start.22 = (f32[112,1]{0,1:T(1,128)S(1)}, f32[112,1]{0,1:T(1,128)S(1)}, u32[]{:S(2)}, u32[]{:S(2)}) collective-permute-start(f32[112,1]{0,1:T(1,128)S(1)} %get-tuple-element.82), channel_id=1, source_target_pairs={{4,0},{8,4},{12,8},{5,1},{9,5},{13,9},{6,2},{10,6},{14,10},{7,3},{... | collective-permute-start | bytes 1352 | tf_op jit(solution)/shard_map/ppermute | solution.py:24
  377.3 68.9 %collective-permute-start.23 = (f32[112,1]{0,1:T(1,128)S(1)}, f32[112,1]{0,1:T(1,128)S(1)}, u32[]{:S(2)}, u32[]{:S(2)}) collective-permute-start(f32[112,1]{0,1:T(1,128)S(1)} %get-tuple-element.83), channel_id=1, source_target_pairs={{0,4},{4,8},{8,12},{1,5},{5,9},{9,13},{2,6},{6,10},{10,14},{3,7},{... | collective-permute-start | bytes 1352 | tf_op jit(solution)/shard_map/ppermute | solution.py:21
  484.9 7.0 %collective-permute-start.16 = (f32[16,1,256]{2,1,0:T(1,128)S(1)}, f32[16,1,256]{2,1,0:T(1,128)S(1)}, u32[]{:S(2)}, u32[]{:S(2)}) collective-permute-start(f32[16,1,256]{2,1,0:T(1,128)S(1)} %get-tuple-element.75), channel_id=1, source_target_pairs={{4,0},{8,4},{12,8},{5,1},{9,5},{13,9},{6,2},{10,6},{14,10},{7,3},{... | collective-permute-start | bytes 49160 | tf_op jit(solution)/shard_map/ppermute | solution.py:24
  (32 other events, 844.2 us)
Sparse Core Ops, SparseCore 0:
  119.1 19.7 reduce-scatter.4
  242.5 19.0 reduce-scatter.6
  367.7 19.0 reduce-scatter.8
  492.0 19.1 reduce-scatter.10
where the time goes:
time: 529 us; the launch traced here: 520 us
  matrix products  346 us (65%)
  starting transfers between devices  65.6 us (12%)
  local copies, waits for them, and re-layouts  37.6 us (7%)
  blocking collectives  27 us (5%)
  other arithmetic  18.4 us (3%)
  between operations  16 us (3%)
  waiting for transfers between devices  9.43 us (2%)
    dot_general x4, matrix products, fetch_strip(): pipe_rows = jnp.einsum('po,joc->pjc', owner_hot, values, precision=EXACT)  182 us
    dot_general x4, matrix products, spread_back(): wide = jnp.einsum('po,pjc->joc', owner_hot, per_pipe, precision=EXACT)  149 us
    ppermute x12, starting transfers between devices, extended(): lax.ppermute(lax.slice_in_dim(block, block.shape[dim] - width, None, axis...  45 us
    all_gather x4, blocking collectives, fetch_strip(): strip = lax.all_gather(board_top, ('gy', 'gz'), axis=1, tiled=True)  27 us
    ppermute x12, starting transfers between devices, extended(): lax.ppermute(lax.slice_in_dim(block, 0, width, axis=dim), axis, backward)  20.4 us
    reshape x4, local copies, waits for them, and re-layouts, fetch_strip(): values = node_values(strip).reshape(node_count, owners, tile_cols)  11.6 us
  transfers between devices with their start and end apart: 28, of which 4 were waited for; matrix products, arithmetic and copies ran while one was open for 62% of the time, Pallas kernels for 0%

commit v1 on v0

v1 whole, which is shorter than its diff:
```python
import functools
import math

import jax
import jax.numpy as jnp
from jax import lax
from jax.experimental import pallas as pl
from jax.experimental.pallas import tpu as pltpu
from jax.sharding import PartitionSpec as P

CUBIC_TERM = 0.05
BOARD_SHARE = 0.5
PERIOD_STEPS = 24.0
SLOTS = 32
LOW = 16
LANES = 128
EXACT = lax.Precision.HIGHEST
MESH = pl.DeviceIdType.MESH
F32 = jnp.float32


def power(moment):
    return 1.0 + 0.5 * jnp.sin(2.0 * math.pi / PERIOD_STEPS * moment.astype(F32))


def kernel(
    sizes,
    board,
    coeff,
    source,
    target,
    pipe_temp,
    pipe_target,
    contact,
    owner,
    traits,
    powers,
    board_out,
    pipe_out,
    grad_out,
    x,
    y,
    e,
    perm,
    send_a,
    send_b,
    recv_a,
    recv_b,
    send_c,
    recv_c,
    turned,
    pipes,
    wanted,
    high_part,
    low_part,
    flux,
    column,
    cells_hot,
    differ,
    sums,
    row_send,
    row_recv,
    col_send,
    col_recv,
    end_send,
    end_recv,
    pipe_sems,
    row_sems,
    col_sems,
    end_sems,
):
    gx_count, gz_count, owners = sizes
    layers, rows, cols = board.shape
    pipe_count, nodes = pipe_temp.shape
    per_row = nodes // rows
    slots = owners * SLOTS
    blocks = slots // LANES
    highs = cols // LOW
    gx = lax.axis_index("gx")
    strip = lax.axis_index("gy") * gz_count + lax.axis_index("gz")
    has = (gx > 0, gx < gx_count - 1, strip > 0, strip < owners - 1)

    def at_strip(other):
        return {"gy": other // gz_count, "gz": lax.rem(other, gz_count)}

    gx_near = ({"gx": gx - 1}, {"gx": gx + 1})
    strip_near = (at_strip(strip - 1), at_strip(strip + 1))

    barrier = pltpu.get_barrier_semaphore()
    for side in range(2):

        @pl.when(has[side])
        def _():
            pl.semaphore_signal(barrier, inc=1, device_id=gx_near[side], device_id_type=MESH)

    for d in range(1, owners):
        pl.semaphore_signal(
            barrier, inc=1, device_id=at_strip(lax.rem(strip + d, owners)), device_id_type=MESH
        )

    def halo_copy(send, recv, sems, moment, side, near):
        return pltpu.make_async_remote_copy(
            src_ref=send.at[moment, side],
            dst_ref=recv.at[moment, 1 - side],
            send_sem=sems.at[0, moment, side],
            recv_sem=sems.at[1, moment, 1 - side],
            device_id=near[side],
            device_id_type=MESH,
        )

    def arrival(send, recv, sems, moment, side, near):
        return pltpu.make_async_remote_copy(
            src_ref=send.at[moment, side],
            dst_ref=recv.at[moment, side],
            send_sem=sems.at[0, moment, side],
            recv_sem=sems.at[1, moment, side],
            device_id=near[side],
            device_id_type=MESH,
        )

    board_kinds = (
        (row_send, row_recv, row_sems, gx_near, 0),
        (col_send, col_recv, col_sems, strip_near, 2),
    )
    end_kind = ((end_send, end_recv, end_sems, gx_near, 0),)

    def start(kinds, moment):
        for send, recv, sems, near, base in kinds:
            for side in range(2):

                @pl.when(has[base + side])
                def _():
                    halo_copy(send, recv, sems, moment, side, near).start()

    def await_halo(kinds, moment):
        for send, recv, sems, near, base in kinds:
            for side in range(2):

                @pl.when(has[base + side])
                def _():
                    arrival(send, recv, sems, moment, side, near).wait_recv()

    def await_sent(kinds, moment):
        for send, recv, sems, near, base in kinds:
            for side in range(2):

                @pl.when(has[base + side])
                def _():
                    halo_copy(send, recv, sems, moment, side, near).wait_send()

    for send, recv, sems, near, base in board_kinds:
        for side in range(2):

            @pl.when(jnp.logical_not(has[base + side]))
            def _():
                for moment in range(4):
                    recv[moment, side] = jnp.zeros(recv.shape[2:], F32)

    lane_cols = lax.broadcasted_iota(jnp.int32, (rows, cols), 1)
    row_ids = lax.broadcasted_iota(jnp.int32, (rows, cols), 0)
    lane_one = lax.broadcasted_iota(jnp.int32, (rows, LANES), 1)
    end_rows = lax.broadcasted_iota(jnp.int32, (rows, slots), 0)

    def boundary(field, moment):
        def body(layer, carry):
            low, high = carry
            now = field[layer + 1]
            row_send[moment, 0, pl.ds(layer, 1), :] = now[0:1, :]
            row_send[moment, 1, pl.ds(layer, 1), :] = now[rows - 1 : rows, :]
            mine = lane_one == layer
            low = jnp.where(mine, now[:, 0:1], low)
            high = jnp.where(mine, now[:, cols - 1 : cols], high)
            return low, high

        zero = jnp.zeros((rows, LANES), F32)
        low, high = lax.fori_loop(0, layers, body, (zero, zero))
        col_send[moment, 0] = low
        col_send[moment, 1] = high
        start(board_kinds, moment)

    def laplacian(field, moment, put):
        def body(layer, _):
            now = field[layer + 1]
            above = row_recv[moment, 0, pl.ds(layer, 1), :]
            below = row_recv[moment, 1, pl.ds(layer, 1), :]
            before = pltpu.roll(col_recv[moment, 0], lax.rem(LANES - layer, LANES), 1)
            after = pltpu.roll(col_recv[moment, 1], LANES - 1 - layer, 1)
            if cols > LANES:
                before = jnp.concatenate([before, now[:, LANES:]], axis=1)
                after = jnp.concatenate([now[:, : cols - LANES], after], axis=1)
            up = jnp.where(row_ids == 0, above, pltpu.roll(now, 1, 0))
            down = jnp.where(row_ids == rows - 1, below, pltpu.roll(now, rows - 1, 0))
            left = jnp.where(lane_cols == 0, before, pltpu.roll(now, 1, 1))
            right = jnp.where(lane_cols == cols - 1, after, pltpu.roll(now, cols - 1, 1))
            put(layer, now, (up + down + left + right + field[layer] + field[layer + 2]) - 6.0 * now)
            return 0

        lax.fori_loop(0, layers, body, 0)

    zero_layer = jnp.zeros((rows, cols), F32)
    for field in (x, y, e):
        field[0] = zero_layer
        field[layers + 1] = zero_layer
    sums[...] = jnp.zeros(sums.shape, F32)
    x[1 : layers + 1] = board[...]

    own = owner[...]
    strips = -(-owners // 8) * 8
    strip_ids = lax.broadcasted_iota(jnp.int32, (strips, pipe_count), 0)
    hot = jnp.where(strip_ids == own, 1.0, 0.0).astype(F32)
    earlier = jnp.where(
        lax.broadcasted_iota(jnp.int32, (pipe_count, pipe_count), 0)
        < lax.broadcasted_iota(jnp.int32, (pipe_count, pipe_count), 1),
        1.0,
        0.0,
    ).astype(F32)
    ahead = jnp.dot(hot, earlier, preferred_element_type=F32)
    rank = jnp.sum(hot * ahead, axis=0, keepdims=True)
    place = own * SLOTS + rank.astype(jnp.int32)
    slot_ids = lax.broadcasted_iota(jnp.int32, (slots, pipe_count), 0)
    perm[...] = jnp.where(slot_ids == place, 1.0, 0.0).astype(F32)

    def sort(values):
        return jnp.dot(perm[...], values, precision=EXACT, preferred_element_type=F32)

    near_count = jnp.int32(owners - 1)
    near_count = near_count + jnp.where(has[0], 1, 0) + jnp.where(has[1], 1, 0)
    pl.semaphore_wait(barrier, near_count)
    boundary(x, 0)

    def exchange(send, recv, which):
        copies = []
        for d in range(1, owners):
            other = lax.rem(strip + d, owners)
            copies.append(
                pltpu.make_async_remote_copy(
                    src_ref=send.at[pl.ds(pl.multiple_of(other * SLOTS, SLOTS), SLOTS)],
                    dst_ref=recv.at[pl.ds(pl.multiple_of(strip * SLOTS, SLOTS), SLOTS)],
                    send_sem=pipe_sems.at[0, which, d],
                    recv_sem=pipe_sems.at[1, which, d],
                    device_id=at_strip(other),
                    device_id_type=MESH,
                )
            )
        for copy in copies:
            copy.start()
        here = pl.ds(pl.multiple_of(strip * SLOTS, SLOTS), SLOTS)
        recv[here, :] = send[here, :]
        return copies

    def await_pipes(recv, send, which):
        for d in range(1, owners):
            source_strip = lax.rem(strip + owners - d, owners)
            pltpu.make_async_remote_copy(
                src_ref=send.at[pl.ds(pl.multiple_of(source_strip * SLOTS, SLOTS), SLOTS)],
                dst_ref=recv.at[pl.ds(pl.multiple_of(source_strip * SLOTS, SLOTS), SLOTS)],
                send_sem=pipe_sems.at[0, which, d],
                recv_sem=pipe_sems.at[1, which, d],
                device_id=at_strip(source_strip),
                device_id_type=MESH,
            ).wait_recv()

    send_a[:, 0:nodes] = sort(pipe_temp[...])
    send_a[:, nodes : 2 * nodes] = jnp.dot(
        perm[...], contact[...].astype(F32), preferred_element_type=F32
    )
    send_a[:, 2 * nodes :] = sort(traits[...])
    copies_a = exchange(send_a, recv_a, 0)
    send_b[...] = sort(pipe_target[...])
    copies_b = exchange(send_b, recv_b, 1)

    def forward_put(to):
        def put(layer, now, lap):
            to[layer + 1] = now + coeff[layer] * lap

        return put

    await_halo(board_kinds, 0)
    laplacian(x, 0, forward_put(y))

    def turn(recv, first, put):
        for b in range(blocks):
            turned[...] = recv[b * LANES : (b + 1) * LANES, first : first + nodes].T
            for k in range(per_row):
                if per_row == 1:
                    values = turned[...]
                else:
                    values = turned[pl.ds(k, rows, stride=per_row), :]
                put(k, b, values)

    def put_pipes(k, b, values):
        pipes[k, :, b * LANES : (b + 1) * LANES] = values

    def put_wanted(k, b, values):
        wanted[k, :, b * LANES : (b + 1) * LANES] = values

    def put_column(k, b, values):
        column[k, :, b * LANES : (b + 1) * LANES] = values.astype(jnp.int32)

    await_pipes(recv_a, send_a, 0)
    turn(recv_a, 0, put_pipes)

    def send_ends(moment):
        first = pipes[0, 0:8, :]
        last = pipes[per_row - 1, rows - 8 : rows, :]
        end_send[moment, 0] = first
        end_send[moment, 1] = last
        start(end_kind, moment)

    send_ends(0)
    turn(recv_a, nodes, put_column)
    trait_rows = [
        recv_a[b * LANES : (b + 1) * LANES, 2 * nodes : 2 * nodes + LANES].T[0:8, :]
        for b in range(blocks)
    ]
    trait_rows = jnp.concatenate(trait_rows, axis=1) if blocks > 1 else trait_rows[0]
    gain = trait_rows[0:1, :]
    conduct = trait_rows[1:2, :]

    low_ids = lax.broadcasted_iota(jnp.int32, (LOW, slots), 0)
    high_ids = lax.broadcasted_iota(jnp.int32, (highs, slots), 0)

    def hot_body(row, _):
        for k in range(per_row):
            cell = jnp.bitwise_and(column[k, pl.ds(row, 1), :], LOW - 1)
            cells_hot[row, :, k * slots : (k + 1) * slots] = jnp.where(
                low_ids == cell, 1.0, 0.0
            ).astype(jnp.bfloat16)
        return 0

    lax.fori_loop(0, rows, hot_body, 0)

    def spread():
        high_part[...] = flux[...].astype(jnp.bfloat16).astype(F32)
        low_part[...] = flux[...] - high_part[...]

        def one_row(row):
            parts = []
            for k in range(per_row):
                mine = high_ids == jnp.right_shift(column[k, pl.ds(row, 1), :], 4)
                top = jnp.where(mine, high_part[k, pl.ds(row, 1), :], 0.0)
                rest = jnp.where(mine, low_part[k, pl.ds(row, 1), :], 0.0)
                parts.append(jnp.concatenate([top, rest], axis=0).astype(jnp.bfloat16))
            hot_values = jnp.concatenate(parts, axis=1)
            both = lax.dot_general(
                hot_values,
                cells_hot[row],
                (((1,), (1,)), ((), ())),
                preferred_element_type=F32,
            )
            sums[pl.ds(pl.multiple_of(row * highs, highs), highs), 0:LOW] = both[:highs] + both[highs:]

        def body(step, _):
            for part in range(4):
                one_row(step * 4 + part)
            return 0

        lax.fori_loop(0, rows // 4, body, 0)
        pieces = []
        per_lane = LANES // LOW
        for half in range(cols // LANES):
            total = sums[pl.ds(half * per_lane, rows, stride=highs), :]
            for h in range(1, per_lane):
                total = total + pltpu.roll(
                    sums[pl.ds(half * per_lane + h, rows, stride=highs), :], h * LOW, 1
                )
            pieces.append(total)
        return jnp.concatenate(pieces, axis=1) if len(pieces) > 1 else pieces[0]

    def fetch(field, k):
        out = []
        for b in range(blocks):
            cell = column[k, :, b * LANES : (b + 1) * LANES]
            within = jnp.bitwise_and(cell, LANES - 1)
            which = jnp.right_shift(cell, 7)
            found = None
            for half in range(cols // LANES):
                table = field[1, :, half * LANES : (half + 1) * LANES]
                values = jnp.take_along_axis(table, within, axis=1, mode="promise_in_bounds")
                found = values if found is None else jnp.where(which == half, values, found)
            out.append(found)
        return jnp.concatenate(out, axis=1) if blocks > 1 else out[0]

    def chain_next(moment, sign):
        await_halo(end_kind, moment)
        planes = [pipes[k] for k in range(per_row)]
        first, last = planes[0], planes[-1]
        low = jnp.where(has[0], end_recv[moment, 0, 7:8, :], first[0:1, :])
        high = jnp.where(has[1], end_recv[moment, 1, 0:1, :], last[rows - 1 : rows, :])
        previous = jnp.where(end_rows == 0, low, pltpu.roll(last, 1, 0))
        following = jnp.where(end_rows == rows - 1, high, pltpu.roll(first, rows - 1, 0))
        for k in range(per_row):
            now = planes[k]
            left = planes[k - 1] if k > 0 else previous
            right = planes[k + 1] if k < per_row - 1 else following
            pipes[k] = now + conduct * ((right - now) + (left - now)) + sign * flux[k]

    def couple(field, moment):
        for k in range(per_row):
            apart = pipes[k] - fetch(field, k)
            differ[moment, k] = apart
            flux[k] = gain * (apart + CUBIC_TERM * apart * apart * apart)

    def couple_back(field, moment):
        for k in range(per_row):
            apart = differ[moment, k]
            weight = gain * (1.0 + 3.0 * CUBIC_TERM * apart * apart)
            flux[k] = (BOARD_SHARE * fetch(field, k) - pipes[k]) * weight

    couple(x, 0)
    chain_next(0, -1.0)
    send_ends(1)
    y[1] = y[1] + powers[0:1, :] * source[...] + BOARD_SHARE * spread()
    boundary(y, 1)

    couple(y, 1)
    chain_next(1, -1.0)
    await_pipes(recv_b, send_b, 1)
    turn(recv_b, 0, put_wanted)
    for k in range(per_row):
        pipes[k] = pipes[k] - wanted[k]
    send_ends(2)
    deposit = spread()
    await_halo(board_kinds, 1)

    def seed_put(layer, now, lap):
        x[layer + 1] = now + coeff[layer] * lap - target[layer]

    laplacian(y, 1, seed_put)
    x[1] = x[1] + powers[1:2, :] * source[...] + BOARD_SHARE * deposit
    grad_out[...] = powers[1:2, :] * x[1]

    def weigh(layer, _):
        e[layer + 1] = coeff[layer] * x[layer + 1]
        return 0

    lax.fori_loop(0, layers, weigh, 0)
    boundary(e, 2)

    couple_back(x, 1)
    chain_next(2, 1.0)
    send_ends(3)
    deposit = spread()
    await_halo(board_kinds, 2)

    def back_put(layer, now, lap):
        y[layer + 1] = x[layer + 1] + lap

    laplacian(e, 2, back_put)
    y[1] = y[1] - deposit
    grad_out[...] = grad_out[...] + powers[0:1, :] * y[1]

    def weigh_again(layer, _):
        e[layer + 1] = coeff[layer] * y[layer + 1]
        return 0

    lax.fori_loop(0, layers, weigh_again, 0)
    boundary(e, 3)

    couple_back(y, 0)
    chain_next(3, 1.0)
    for b in range(blocks):
        for k in range(per_row):
            values = pipes[k, :, b * LANES : (b + 1) * LANES]
            if per_row == 1:
                turned[...] = values
            else:
                turned[pl.ds(k, rows, stride=per_row), :] = values
        send_c[b * LANES : (b + 1) * LANES, :] = turned[...].T
    copies_c = exchange(send_c, recv_c, 2)
    deposit = spread()
    await_halo(board_kinds, 3)

    def last_put(layer, now, lap):
        board_out[layer] = y[layer + 1] + lap

    laplacian(e, 3, last_put)
    board_out[0] = board_out[0] - deposit
    await_pipes(recv_c, send_c, 2)
    pipe_out[...] = lax.dot_general(
        perm[...],
        recv_c[...],
        (((0,), (0,)), ((), ())),
        precision=EXACT,
        preferred_element_type=F32,
    )

    for moment in range(4):
        await_sent(board_kinds, moment)
        await_sent(end_kind, moment)
    for copy in copies_a + copies_b + copies_c:
        copy.wait_send()


def solution(mesh):
    gx_count = mesh.shape["gx"]
    gz_count = mesh.shape["gz"]
    owners = mesh.shape["gy"] * gz_count

    def local(
        board_temp,
        board_coeff,
        source,
        board_target,
        pipe_temp,
        pipe_target,
        pipe_cond,
        contact_gain,
        contact_col,
        pipe_owner,
        step_index,
    ):
        layers, rows, cols = board_temp.shape
        pipe_count, nodes = pipe_temp.shape
        per_row = nodes // rows
        slots = owners * SLOTS
        highs = cols // LOW
        traits = jnp.concatenate(
            [
                contact_gain[:, None],
                pipe_cond[:, None],
                jnp.zeros((pipe_count, LANES - 2), F32),
            ],
            axis=1,
        )
        moments = step_index[0] + jnp.arange(2, dtype=jnp.int32)
        powers = jnp.broadcast_to(power(moments)[:, None], (2, cols))
        field = pltpu.VMEM((layers + 2, rows, cols), F32)
        planes = pltpu.VMEM((per_row, rows, slots), F32)
        vmem = pl.BlockSpec(memory_space=pltpu.VMEM)
        return pl.pallas_call(
            functools.partial(kernel, (gx_count, gz_count, owners)),
            out_shape=(
                jax.ShapeDtypeStruct(board_temp.shape, F32),
                jax.ShapeDtypeStruct(pipe_temp.shape, F32),
                jax.ShapeDtypeStruct(source.shape, F32),
            ),
            in_specs=[vmem] * 10,
            out_specs=[vmem] * 3,
            scratch_shapes=[
                field,
                field,
                field,
                pltpu.VMEM((slots, pipe_count), F32),
                pltpu.VMEM((slots, 2 * nodes + LANES), F32),
                pltpu.VMEM((slots, nodes), F32),
                pltpu.VMEM((slots, 2 * nodes + LANES), F32),
                pltpu.VMEM((slots, nodes), F32),
                pltpu.VMEM((slots, nodes), F32),
                pltpu.VMEM((slots, nodes), F32),
                pltpu.VMEM((nodes, LANES), F32),
                planes,
                planes,
                planes,
                planes,
                planes,
                pltpu.VMEM((per_row, rows, slots), jnp.int32),
                pltpu.VMEM((rows, LOW, per_row * slots), jnp.bfloat16),
                pltpu.VMEM((2, per_row, rows, slots), F32),
                pltpu.VMEM((rows * highs, LANES), F32),
                pltpu.VMEM((4, 2, layers, cols), F32),
                pltpu.VMEM((4, 2, layers, cols), F32),
                pltpu.VMEM((4, 2, rows, LANES), F32),
                pltpu.VMEM((4, 2, rows, LANES), F32),
                pltpu.VMEM((4, 2, 8, slots), F32),
                pltpu.VMEM((4, 2, 8, slots), F32),
                pltpu.SemaphoreType.DMA((2, 3, owners)),
                pltpu.SemaphoreType.DMA((2, 4, 2)),
                pltpu.SemaphoreType.DMA((2, 4, 2)),
                pltpu.SemaphoreType.DMA((2, 4, 2)),
            ],
            compiler_params=pltpu.CompilerParams(
                collective_id=0, has_side_effects=True, vmem_limit_bytes=48 * 1024 * 1024
            ),
        )(
            board_temp,
            board_coeff,
            source,
            board_target,
            pipe_temp,
            pipe_target,
            contact_col,
            pipe_owner[None, :],
            traits,
            powers,
        )

    placed = (
        P("group", "gx", ("gy", "gz")),
        P("group", "gx", ("gy", "gz")),
        P(("group", "gx"), ("gy", "gz")),
        P("group", "gx", ("gy", "gz")),
        P(("group", "gy", "gz"), "gx"),
        P(("group", "gy", "gz"), "gx"),
        P(("group", "gy", "gz")),
        P(("group", "gy", "gz")),
        P(("group", "gy", "gz"), "gx"),
        P(("group", "gy", "gz")),
        P("group"),
    )
    return jax.shard_map(
        local,
        mesh=mesh,
        in_specs=placed,
        out_specs=(
            P("group", "gx", ("gy", "gz")),
            P(("group", "gy", "gz"), "gx"),
            P(("group", "gx"), ("gy", "gz")),
        ),
        check_vma=False,
    )
```

time: 529 us -> 57.8 us (0.11); the launches traced: 520 us -> 57.5 us
  matrix products: 346 us -> 0 us
  starting transfers between devices: 65.6 us -> 0 us
  Pallas kernels: 0 us -> 45.7 us
  local copies, waits for them, and re-layouts: 37.6 us -> 10.2 us
  blocking collectives: 27 us -> 0 us
  other arithmetic: 18.4 us -> 0.13 us
  between operations: 16 us -> 1.38 us
  waiting for transfers between devices: 9.43 us -> 0 us
    dot_general x16 -> x0, matrix products: 346 us -> none  [the longest x4 182 us: fetch_strip(): pipe_rows = jnp.einsum('po,joc->pjc', owner_hot, values, precision=EXACT)]
    ppermute x24 -> x0, starting transfers between devices: 65.4 us -> none  [the longest x12 45 us: extended(): lax.ppermute(lax.slice_in_dim(block, block.shape[dim] - width, None, axis...]
    pallas_call x0 -> x1, Pallas kernels: none -> 45.7 us  [local(): pl.pallas_call(functools.partial(kernel, (gx_count, gz_count, owners)), o...]
    all_gather x4 -> x0, blocking collectives: 27 us -> none  [fetch_strip(): strip = lax.all_gather(board_top, ('gy', 'gz'), axis=1, tiled=True)]
    add x8 -> x1, other arithmetic: 13.5 us -> 0.05 us  [power(): 1.0 + 0.5 * jnp.sin(2.0 * math.pi / PERIOD_STEPS * moment.astype(F32))]
    slice x22 -> x0, local copies, waits for them, and re-layouts: 12.1 us -> none  [the longest x12 9.18 us: extended(): lax.slice_in_dim(block, 0, width, axis=dim)]
    reshape x4 -> x0, local copies, waits for them, and re-layouts: 11.6 us -> none  [fetch_strip(): values = node_values(strip).reshape(node_count, owners, tile_cols)]
    reduce_scatter x4 -> x0, waiting for transfers between devices: 9.3 us -> none  [spread_back(): return lax.psum_scatter(wide, ('gy', 'gz'), scatter_dimension=1, tiled=True)]
  transfers between devices with their start and end apart: 28 -> 0, of which waited for: 4 -> 0; matrix products, arithmetic and copies ran while one was open for 62% -> 0% of each run, Pallas kernels for 0% -> 0%
where the time goes in v1:
time: 57.8 us; the launch traced here: 57.5 us
  Pallas kernels  45.7 us (79%)
  local copies, waits for them, and re-layouts  10.2 us (18%)
  between operations  1.38 us (2%)
    pallas_call x1, Pallas kernels, local(): pl.pallas_call(functools.partial(kernel, (gx_count, gz_count, owners)), o...  45.7 us
    unnamed x19, local copies, waits for them, and re-layouts  8.57 us

profile of v1, /device:TPU:1, one launch (start us, length us, event | category | flops | bytes accessed | tf_op | source)
XLA Modules:
  0.0 57.5 jit_solution(3870139090606147666)
XLA Ops:
  0.6 0.0 copy-start.3
  1.4 0.1 pad.2.clone
  1.5 0.1 broadcast_in_dim.22.powers
  1.5 0.8 %copy.15 = f32[112,1]{1,0:T(8,128)S(1)} copy(f32[112,1]{0,1:T(1,128)} %bitcast.6) | data formatting | bytes 896 | tf_op jit(solution)/shard_map/broadcast_in_dim | solution.py:521
  2.3 0.8 %copy.14 = f32[112,1]{1,0:T(8,128)S(1)} copy(f32[112,1]{0,1:T(1,128)} %bitcast.7) | data formatting | bytes 896 | tf_op jit(solution)/shard_map/broadcast_in_dim | solution.py:520
  3.0 0.0 copy-start.6
  3.0 0.0 copy-start.7
  3.1 0.1 maximum_maximum_fusion.traits
  3.2 0.0 copy-done.3
  3.2 0.7 %copy-done.6 = f32[64,256]{1,0:T(8,128)S(1)} copy-done((f32[64,256]{1,0:T(8,128)S(1)}, f32[64,256]{1,0:T(8,128)}, u32[]{:S(2)}) %copy-start.6) | copy-done | bytes 65560
  3.9 0.0 copy-done.7
  3.9 0.0 copy-start
  3.9 1.2 %copy-done = f32[16,64,256]{2,1,0:T(8,128)S(1)} copy-done((f32[16,64,256]{2,1,0:T(8,128)S(1)}, f32[16,64,256]{2,1,0:T(8,128)}, u32[]{:S(2)}) %copy-start) | copy-done | bytes 1048600
  5.1 0.0 copy-start.1
  5.1 1.2 %copy-done.1 = f32[16,64,256]{2,1,0:T(8,128)S(1)} copy-done((f32[16,64,256]{2,1,0:T(8,128)S(1)}, f32[16,64,256]{2,1,0:T(8,128)}, u32[]{:S(2)}) %copy-start.1) | copy-done | bytes 1048600
  6.3 0.0 copy-start.2
  6.3 1.2 %copy-done.2 = f32[16,64,256]{2,1,0:T(8,128)S(1)} copy-done((f32[16,64,256]{2,1,0:T(8,128)S(1)}, f32[16,64,256]{2,1,0:T(8,128)}, u32[]{:S(2)}) %copy-start.2) | copy-done | bytes 1048600
  7.6 0.0 copy-start.4
  7.6 0.9 %copy-done.4 = f32[112,512]{1,0:T(8,128)S(1)} copy-done((f32[112,512]{1,0:T(8,128)S(1)}, f32[112,512]{1,0:T(8,128)}, u32[]{:S(2)}) %copy-start.4) | copy-done | bytes 229400
  8.5 0.9 %copy-done.5 = s32[112,512]{1,0:T(8,128)S(1)} copy-done((s32[112,512]{1,0:T(8,128)S(1)}, s32[112,512]{1,0:T(8,128)}, u32[]{:S(2)}) %copy-start.5) | copy-done | bytes 229400
  9.4 45.7 %shard_map.130 = (f32[16,64,256]{2,1,0:T(8,128)S(1)}, f32[112,512]{1,0:T(8,128)S(1)}, f32[64,256]{1,0:T(8,128)S(1)}) custom-call(f32[16,64,256]{2,1,0:T(8,128)S(1)} %copy-done, f32[16,64,256]{2,1,0:T(8,128)S(1)} %copy-done.1, f32[64,256]{1,0:T(8,128)S(1)} %copy-done.6, f32[16,64,256]{2,1,0:T(8,128)S(1)} %copy-done.2, f32[112,512]{1,0:T(8,128)S(1)} %copy-done.3, ...), custom_call_target="tpu_custom_call" | custom-call | tf_op jit(solution)/shard_map/pallas_call | solution.py:531
  55.2 1.0 %copy.20 = f32[16,64,256]{2,1,0:T(8,128)} copy(f32[16,64,256]{2,1,0:T(8,128)S(1)} %get-tuple-element.6) | data formatting | bytes 2097152
  56.2 0.7 %copy.21 = f32[112,512]{1,0:T(8,128)} copy(f32[112,512]{1,0:T(8,128)S(1)} %get-tuple-element.7) | data formatting | bytes 458752
  56.8 0.6 %copy.22 = f32[64,256]{1,0:T(8,128)} copy(f32[64,256]{1,0:T(8,128)S(1)} %get-tuple-element.8) | data formatting | bytes 131072
  (3 shorter events, 0.0 us)
Async XLA Ops:
  0.6 2.5 %copy-start.3 = (f32[112,512]{1,0:T(8,128)S(1)}, f32[112,512]{1,0:T(8,128)}, u32[]{:S(2)}) copy-start(f32[112,512]{1,0:T(8,128)} %pipe_temp.1) | copy-start | bytes 688132
  3.0 0.8 %copy-start.6 = (f32[64,256]{1,0:T(8,128)S(1)}, f32[64,256]{1,0:T(8,128)}, u32[]{:S(2)}) copy-start(f32[64,256]{1,0:T(8,128)} %source.1) | copy-start | bytes 196612
  3.0 0.8 %copy-start.7 = (s32[112]{0:T(128)S(1)}, s32[112]{0:T(128)}, u32[]{:S(2)}) copy-start(s32[112]{0:T(128)} %param.20) | copy-start | bytes 1348
  3.9 1.2 %copy-start = (f32[16,64,256]{2,1,0:T(8,128)S(1)}, f32[16,64,256]{2,1,0:T(8,128)}, u32[]{:S(2)}) copy-start(f32[16,64,256]{2,1,0:T(8,128)} %board.1) | copy-start | bytes 3145732
  5.1 1.2 %copy-start.1 = (f32[16,64,256]{2,1,0:T(8,128)S(1)}, f32[16,64,256]{2,1,0:T(8,128)}, u32[]{:S(2)}) copy-start(f32[16,64,256]{2,1,0:T(8,128)} %coeff.1) | copy-start | bytes 3145732
  6.3 1.2 %copy-start.2 = (f32[16,64,256]{2,1,0:T(8,128)S(1)}, f32[16,64,256]{2,1,0:T(8,128)}, u32[]{:S(2)}) copy-start(f32[16,64,256]{2,1,0:T(8,128)} %target.1) | copy-start | bytes 3145732
  7.6 0.9 %copy-start.4 = (f32[112,512]{1,0:T(8,128)S(1)}, f32[112,512]{1,0:T(8,128)}, u32[]{:S(2)}) copy-start(f32[112,512]{1,0:T(8,128)} %pipe_target.1) | copy-start | bytes 688132
  8.5 0.9 %copy-start.5 = (s32[112,512]{1,0:T(8,128)S(1)}, s32[112,512]{1,0:T(8,128)}, u32[]{:S(2)}) copy-start(s32[112,512]{1,0:T(8,128)} %contact.1) | copy-start | bytes 688132

commit v2 on v1

--- a/solution.py
+++ b/solution.py
@@ -25,19 +25,29 @@
 
 def kernel(
     sizes,
-    board,
+    board_hbm,
+    coeff_hbm,
+    source_hbm,
+    target_hbm,
+    pipe_temp_hbm,
+    pipe_target_hbm,
+    contact_hbm,
+    owner,
+    gains,
+    conds,
+    powers,
+    board_out,
+    pipe_out,
+    grad_out,
     coeff,
     source,
     target,
     pipe_temp,
     pipe_target,
     contact,
-    owner,
-    traits,
-    powers,
-    board_out,
-    pipe_out,
-    grad_out,
+    in_sems,
+    trait_send,
+    trait_recv,
     x,
     y,
     e,
@@ -70,7 +80,7 @@
     end_sems,
 ):
     gx_count, gz_count, owners = sizes
-    layers, rows, cols = board.shape
+    layers, rows, cols = board_hbm.shape
     pipe_count, nodes = pipe_temp.shape
     per_row = nodes // rows
     slots = owners * SLOTS
@@ -79,6 +89,23 @@
     gx = lax.axis_index("gx")
     strip = lax.axis_index("gy") * gz_count + lax.axis_index("gz")
     has = (gx > 0, gx < gx_count - 1, strip > 0, strip < owners - 1)
+
+    loads = [
+        pltpu.make_async_copy(there, here, in_sems.at[i])
+        for i, (there, here) in enumerate(
+            (
+                (pipe_temp_hbm, pipe_temp),
+                (contact_hbm, contact),
+                (board_hbm, x.at[pl.ds(1, layers)]),
+                (coeff_hbm, coeff),
+                (pipe_target_hbm, pipe_target),
+                (source_hbm, source),
+                (target_hbm, target),
+            )
+        )
+    ]
+    for load in loads:
+        load.start()
 
     def at_strip(other):
         return {"gy": other // gz_count, "gz": lax.rem(other, gz_count)}
@@ -160,6 +187,16 @@
     row_ids = lax.broadcasted_iota(jnp.int32, (rows, cols), 0)
     lane_one = lax.broadcasted_iota(jnp.int32, (rows, LANES), 1)
     end_rows = lax.broadcasted_iota(jnp.int32, (rows, slots), 0)
+
+    def over_layers(body, carry, together):
+        together = math.gcd(layers, together)
+
+        def several(step, inner):
+            for part in range(together):
+                inner = body(step * together + part, inner)
+            return inner
+
+        return lax.fori_loop(0, layers // together, several, carry)
 
     def boundary(field, moment):
         def body(layer, carry):
@@ -173,7 +210,7 @@
             return low, high
 
         zero = jnp.zeros((rows, LANES), F32)
-        low, high = lax.fori_loop(0, layers, body, (zero, zero))
+        low, high = over_layers(body, (zero, zero), 8)
         col_send[moment, 0] = low
         col_send[moment, 1] = high
         start(board_kinds, moment)
@@ -195,14 +232,13 @@
             put(layer, now, (up + down + left + right + field[layer] + field[layer + 2]) - 6.0 * now)
             return 0
 
-        lax.fori_loop(0, layers, body, 0)
+        over_layers(body, 0, 4)
 
     zero_layer = jnp.zeros((rows, cols), F32)
     for field in (x, y, e):
         field[0] = zero_layer
         field[layers + 1] = zero_layer
     sums[...] = jnp.zeros(sums.shape, F32)
-    x[1 : layers + 1] = board[...]
 
     own = owner[...]
     strips = -(-owners // 8) * 8
@@ -226,13 +262,12 @@
     near_count = jnp.int32(owners - 1)
     near_count = near_count + jnp.where(has[0], 1, 0) + jnp.where(has[1], 1, 0)
     pl.semaphore_wait(barrier, near_count)
-    boundary(x, 0)
 
     def exchange(send, recv, which):
-        copies = []
+        made = []
         for d in range(1, owners):
             other = lax.rem(strip + d, owners)
-            copies.append(
+            made.append(
                 pltpu.make_async_remote_copy(
                     src_ref=send.at[pl.ds(pl.multiple_of(other * SLOTS, SLOTS), SLOTS)],
                     dst_ref=recv.at[pl.ds(pl.multiple_of(strip * SLOTS, SLOTS), SLOTS)],
@@ -242,11 +277,11 @@
                     device_id_type=MESH,
                 )
             )
-        for copy in copies:
+        for copy in made:
             copy.start()
         here = pl.ds(pl.multiple_of(strip * SLOTS, SLOTS), SLOTS)
         recv[here, :] = send[here, :]
-        return copies
+        return made
 
     def await_pipes(recv, send, which):
         for d in range(1, owners):
@@ -260,14 +295,44 @@
                 device_id_type=MESH,
             ).wait_recv()
 
-    send_a[:, 0:nodes] = sort(pipe_temp[...])
-    send_a[:, nodes : 2 * nodes] = jnp.dot(
-        perm[...], contact[...].astype(F32), preferred_element_type=F32
+    loads[0].wait()
+    send_a[0] = sort(pipe_temp[...])
+    copies = exchange(send_a.at[0], recv_a.at[0], 0)
+    loads[1].wait()
+    send_a[1] = jnp.dot(perm[...], contact[...].astype(F32), preferred_element_type=F32)
+    copies += exchange(send_a.at[1], recv_a.at[1], 1)
+    trait_rows = jnp.concatenate(
+        [gains[...], conds[...], jnp.zeros((6, pipe_count), F32)], axis=0
     )
-    send_a[:, 2 * nodes :] = sort(traits[...])
-    copies_a = exchange(send_a, recv_a, 0)
+    trait_send[...] = lax.dot_general(
+        trait_rows,
+        perm[...],
+        (((1,), (1,)), ((), ())),
+        precision=EXACT,
+        preferred_element_type=F32,
+    )
+    trait_copies = []
+    for d in range(1, owners):
+        trait_copies.append(
+            pltpu.make_async_remote_copy(
+                src_ref=trait_send,
+                dst_ref=trait_recv.at[strip],
+                send_sem=pipe_sems.at[0, 4, d],
+                recv_sem=pipe_sems.at[1, 4, d],
+                device_id=at_strip(lax.rem(strip + d, owners)),
+                device_id_type=MESH,
+            )
+        )
+    for copy in trait_copies:
+        copy.start()
+    copies += trait_copies
+    trait_recv[strip] = trait_send[...]
+    loads[2].wait()
+    boundary(x, 0)
+    loads[4].wait()
     send_b[...] = sort(pipe_target[...])
-    copies_b = exchange(send_b, recv_b, 1)
+    copies += exchange(send_b, recv_b, 2)
+    loads[3].wait()
 
     def forward_put(to):
         def put(layer, now, lap):
@@ -278,9 +343,9 @@
     await_halo(board_kinds, 0)
     laplacian(x, 0, forward_put(y))
 
-    def turn(recv, first, put):
+    def turn(recv, put):
         for b in range(blocks):
-            turned[...] = recv[b * LANES : (b + 1) * LANES, first : first + nodes].T
+            turned[...] = recv[b * LANES : (b + 1) * LANES, :].T
             for k in range(per_row):
                 if per_row == 1:
                     values = turned[...]
@@ -297,8 +362,8 @@
     def put_column(k, b, values):
         column[k, :, b * LANES : (b + 1) * LANES] = values.astype(jnp.int32)
 
-    await_pipes(recv_a, send_a, 0)
-    turn(recv_a, 0, put_pipes)
+    await_pipes(recv_a.at[0], send_a.at[0], 0)
+    turn(recv_a.at[0], put_pipes)
 
     def send_ends(moment):
         first = pipes[0, 0:8, :]
@@ -308,12 +373,24 @@
         start(end_kind, moment)
 
     send_ends(0)
-    turn(recv_a, nodes, put_column)
-    trait_rows = [
-        recv_a[b * LANES : (b + 1) * LANES, 2 * nodes : 2 * nodes + LANES].T[0:8, :]
-        for b in range(blocks)
-    ]
-    trait_rows = jnp.concatenate(trait_rows, axis=1) if blocks > 1 else trait_rows[0]
+    await_pipes(recv_a.at[1], send_a.at[1], 1)
+    turn(recv_a.at[1], put_column)
+    for d in range(1, owners):
+        source_strip = lax.rem(strip + owners - d, owners)
+        pltpu.make_async_remote_copy(
+            src_ref=trait_send,
+            dst_ref=trait_recv.at[source_strip],
+            send_sem=pipe_sems.at[0, 4, d],
+            recv_sem=pipe_sems.at[1, 4, d],
+            device_id=at_strip(source_strip),
+            device_id_type=MESH,
+        ).wait_recv()
+    trait_lane = lax.broadcasted_iota(jnp.int32, (8, slots), 1)
+    trait_rows = jnp.zeros((8, slots), F32)
+    for other in range(owners):
+        shift = lax.rem((other + owners - strip) * SLOTS, slots)
+        mine = (trait_lane >= other * SLOTS) & (trait_lane < (other + 1) * SLOTS)
+        trait_rows = jnp.where(mine, pltpu.roll(trait_recv[other], shift, 1), trait_rows)
     gain = trait_rows[0:1, :]
     conduct = trait_rows[1:2, :]
 
@@ -333,6 +410,8 @@
     def spread():
         high_part[...] = flux[...].astype(jnp.bfloat16).astype(F32)
         low_part[...] = flux[...] - high_part[...]
+
+        together = math.gcd(rows, 8)
 
         def one_row(row):
             parts = []
@@ -351,11 +430,11 @@
             sums[pl.ds(pl.multiple_of(row * highs, highs), highs), 0:LOW] = both[:highs] + both[highs:]
 
         def body(step, _):
-            for part in range(4):
-                one_row(step * 4 + part)
+            for part in range(together):
+                one_row(step * together + part)
             return 0
 
-        lax.fori_loop(0, rows // 4, body, 0)
+        lax.fori_loop(0, rows // together, body, 0)
         pieces = []
         per_lane = LANES // LOW
         for half in range(cols // LANES):
@@ -410,18 +489,20 @@
     couple(x, 0)
     chain_next(0, -1.0)
     send_ends(1)
+    loads[5].wait()
     y[1] = y[1] + powers[0:1, :] * source[...] + BOARD_SHARE * spread()
     boundary(y, 1)
 
     couple(y, 1)
     chain_next(1, -1.0)
-    await_pipes(recv_b, send_b, 1)
-    turn(recv_b, 0, put_wanted)
+    await_pipes(recv_b, send_b, 2)
+    turn(recv_b, put_wanted)
     for k in range(per_row):
         pipes[k] = pipes[k] - wanted[k]
     send_ends(2)
     deposit = spread()
     await_halo(board_kinds, 1)
+    loads[6].wait()
 
     def seed_put(layer, now, lap):
         x[layer + 1] = now + coeff[layer] * lap - target[layer]
@@ -434,7 +515,7 @@
         e[layer + 1] = coeff[layer] * x[layer + 1]
         return 0
 
-    lax.fori_loop(0, layers, weigh, 0)
+    over_layers(weigh, 0, 4)
     boundary(e, 2)
 
     couple_back(x, 1)
@@ -454,7 +535,7 @@
         e[layer + 1] = coeff[layer] * y[layer + 1]
         return 0
 
-    lax.fori_loop(0, layers, weigh_again, 0)
+    over_layers(weigh_again, 0, 4)
     boundary(e, 3)
 
     couple_back(y, 0)
@@ -467,7 +548,7 @@
             else:
                 turned[pl.ds(k, rows, stride=per_row), :] = values
         send_c[b * LANES : (b + 1) * LANES, :] = turned[...].T
-    copies_c = exchange(send_c, recv_c, 2)
+    copies += exchange(send_c, recv_c, 3)
     deposit = spread()
     await_halo(board_kinds, 3)
 
@@ -476,7 +557,7 @@
 
     laplacian(e, 3, last_put)
     board_out[0] = board_out[0] - deposit
-    await_pipes(recv_c, send_c, 2)
+    await_pipes(recv_c, send_c, 3)
     pipe_out[...] = lax.dot_general(
         perm[...],
         recv_c[...],
@@ -488,7 +569,7 @@
     for moment in range(4):
         await_sent(board_kinds, moment)
         await_sent(end_kind, moment)
-    for copy in copies_a + copies_b + copies_c:
+    for copy in copies:
         copy.wait_send()
 
 
@@ -515,19 +596,12 @@
         per_row = nodes // rows
         slots = owners * SLOTS
         highs = cols // LOW
-        traits = jnp.concatenate(
-            [
-                contact_gain[:, None],
-                pipe_cond[:, None],
-                jnp.zeros((pipe_count, LANES - 2), F32),
-            ],
-            axis=1,
-        )
         moments = step_index[0] + jnp.arange(2, dtype=jnp.int32)
         powers = jnp.broadcast_to(power(moments)[:, None], (2, cols))
         field = pltpu.VMEM((layers + 2, rows, cols), F32)
         planes = pltpu.VMEM((per_row, rows, slots), F32)
         vmem = pl.BlockSpec(memory_space=pltpu.VMEM)
+        hbm = pl.BlockSpec(memory_space=pltpu.HBM)
         return pl.pallas_call(
             functools.partial(kernel, (gx_count, gz_count, owners)),
             out_shape=(
@@ -535,16 +609,25 @@
                 jax.ShapeDtypeStruct(pipe_temp.shape, F32),
                 jax.ShapeDtypeStruct(source.shape, F32),
             ),
-            in_specs=[vmem] * 10,
+            in_specs=[hbm] * 7 + [vmem] * 4,
             out_specs=[vmem] * 3,
             scratch_shapes=[
+                pltpu.VMEM(board_coeff.shape, F32),
+                pltpu.VMEM(source.shape, F32),
+                pltpu.VMEM(board_target.shape, F32),
+                pltpu.VMEM(pipe_temp.shape, F32),
+                pltpu.VMEM(pipe_target.shape, F32),
+                pltpu.VMEM(contact_col.shape, jnp.int32),
+                pltpu.SemaphoreType.DMA((7,)),
+                pltpu.VMEM((8, slots), F32),
+                pltpu.VMEM((owners, 8, slots), F32),
                 field,
                 field,
                 field,
                 pltpu.VMEM((slots, pipe_count), F32),
-                pltpu.VMEM((slots, 2 * nodes + LANES), F32),
+                pltpu.VMEM((2, slots, nodes), F32),
                 pltpu.VMEM((slots, nodes), F32),
-                pltpu.VMEM((slots, 2 * nodes + LANES), F32),
+                pltpu.VMEM((2, slots, nodes), F32),
                 pltpu.VMEM((slots, nodes), F32),
                 pltpu.VMEM((slots, nodes), F32),
                 pltpu.VMEM((slots, nodes), F32),
@@ -564,7 +647,7 @@
                 pltpu.VMEM((4, 2, rows, LANES), F32),
                 pltpu.VMEM((4, 2, 8, slots), F32),
                 pltpu.VMEM((4, 2, 8, slots), F32),
-                pltpu.SemaphoreType.DMA((2, 3, owners)),
+                pltpu.SemaphoreType.DMA((2, 5, owners)),
                 pltpu.SemaphoreType.DMA((2, 4, 2)),
                 pltpu.SemaphoreType.DMA((2, 4, 2)),
                 pltpu.SemaphoreType.DMA((2, 4, 2)),
@@ -581,7 +664,8 @@
             pipe_target,
             contact_col,
             pipe_owner[None, :],
-            traits,
+            contact_gain[None, :],
+            pipe_cond[None, :],
             powers,
         )
 

time: 57.8 us -> 49.7 us (0.86)
  Pallas kernels: 45.7 us -> 37.7 us
    pallas_call x1, Pallas kernels: 45.7 us -> 37.7 us  [local(): pl.pallas_call(functools.partial(kernel, (gx_count, gz_count, owners)), o...]
    unnamed x19 -> x23, local copies, waits for them, and re-layouts: 8.57 us -> 10.2 us
    broadcast_in_dim x3 -> x0, local copies, waits for them, and re-layouts: 1.52 us -> none  [the longest x1 0.76 us: local(): pipe_cond[:, None]]
where the time goes in v2:
time: 49.7 us; the launch traced here: 49.3 us
  Pallas kernels  37.7 us (76%)
  local copies, waits for them, and re-layouts  10.3 us (21%)
  between operations  1.32 us (3%)
    pallas_call x1, Pallas kernels, local(): pl.pallas_call(functools.partial(kernel, (gx_count, gz_count, owners)), o...  37.7 us
    unnamed x23, local copies, waits for them, and re-layouts  10.2 us

profile of v2, /device:TPU:1, one launch (start us, length us, event | category | flops | bytes accessed | tf_op | source)
XLA Modules:
  0.0 49.3 jit_solution(17018579476561765082)
XLA Ops:
  1.3 0.0 copy-start.7
  1.3 0.0 copy-start.8
  1.3 0.0 copy-start.9
  1.4 0.1 broadcast_in_dim.18.powers
  1.4 0.6 %copy-done.7 = s32[112]{0:T(128)S(1)} copy-done((s32[112]{0:T(128)S(1)}, s32[112]{0:T(128)}, u32[]{:S(2)}) %copy-start.7) | copy-done | bytes 472
  2.0 0.0 copy-done.8
  2.0 0.0 copy-done.9
  2.0 0.0 copy-start
  2.0 1.2 %copy-done = f32[16,64,256]{2,1,0:T(8,128)S(1)} copy-done((f32[16,64,256]{2,1,0:T(8,128)S(1)}, f32[16,64,256]{2,1,0:T(8,128)}, u32[]{:S(2)}) %copy-start) | copy-done | bytes 1048600
  3.2 0.0 copy-start.1
  3.2 1.2 %copy-done.1 = f32[16,64,256]{2,1,0:T(8,128)S(1)} copy-done((f32[16,64,256]{2,1,0:T(8,128)S(1)}, f32[16,64,256]{2,1,0:T(8,128)}, u32[]{:S(2)}) %copy-start.1) | copy-done | bytes 1048600
  4.5 0.0 copy-start.2
  4.5 1.2 %copy-done.2 = f32[16,64,256]{2,1,0:T(8,128)S(1)} copy-done((f32[16,64,256]{2,1,0:T(8,128)S(1)}, f32[16,64,256]{2,1,0:T(8,128)}, u32[]{:S(2)}) %copy-start.2) | copy-done | bytes 1048600
  5.7 0.0 copy-start.3
  5.7 0.9 %copy-done.3 = f32[112,512]{1,0:T(8,128)S(1)} copy-done((f32[112,512]{1,0:T(8,128)S(1)}, f32[112,512]{1,0:T(8,128)}, u32[]{:S(2)}) %copy-start.3) | copy-done | bytes 229400
  6.6 0.0 copy-start.4
  6.6 0.9 %copy-done.4 = f32[112,512]{1,0:T(8,128)S(1)} copy-done((f32[112,512]{1,0:T(8,128)S(1)}, f32[112,512]{1,0:T(8,128)}, u32[]{:S(2)}) %copy-start.4) | copy-done | bytes 229400
  7.6 0.0 copy-start.5
  7.6 0.9 %copy-done.5 = s32[112,512]{1,0:T(8,128)S(1)} copy-done((s32[112,512]{1,0:T(8,128)S(1)}, s32[112,512]{1,0:T(8,128)}, u32[]{:S(2)}) %copy-start.5) | copy-done | bytes 229400
  8.5 0.8 %copy-done.6 = f32[64,256]{1,0:T(8,128)S(1)} copy-done((f32[64,256]{1,0:T(8,128)S(1)}, f32[64,256]{1,0:T(8,128)}, u32[]{:S(2)}) %copy-start.6) | copy-done | bytes 65560
  9.3 37.7 %shard_map.130 = (f32[16,64,256]{2,1,0:T(8,128)S(1)}, f32[112,512]{1,0:T(8,128)S(1)}, f32[64,256]{1,0:T(8,128)S(1)}) custom-call(f32[16,64,256]{2,1,0:T(8,128)S(1)} %copy-done, f32[16,64,256]{2,1,0:T(8,128)S(1)} %copy-done.1, f32[64,256]{1,0:T(8,128)S(1)} %copy-done.6, f32[16,64,256]{2,1,0:T(8,128)S(1)} %copy-done.2, f32[112,512]{1,0:T(8,128)S(1)} %copy-done.3, ...), custom_call_target="tpu_custom_call" | custom-call | tf_op jit(solution)/shard_map/pallas_call | solution.py:605
  47.1 1.0 %copy.18 = f32[16,64,256]{2,1,0:T(8,128)} copy(f32[16,64,256]{2,1,0:T(8,128)S(1)} %get-tuple-element.6) | data formatting | bytes 2097152
  48.0 0.7 %copy.19 = f32[112,512]{1,0:T(8,128)} copy(f32[112,512]{1,0:T(8,128)S(1)} %get-tuple-element.7) | data formatting | bytes 458752
  48.7 0.6 %copy.20 = f32[64,256]{1,0:T(8,128)} copy(f32[64,256]{1,0:T(8,128)S(1)} %get-tuple-element.8) | data formatting | bytes 131072
  (2 shorter events, 0.0 us)
Async XLA Ops:
  1.3 0.7 %copy-start.7 = (s32[112]{0:T(128)S(1)}, s32[112]{0:T(128)}, u32[]{:S(2)}) copy-start(s32[112]{0:T(128)} %param.20) | copy-start | bytes 1348
  1.3 0.7 %copy-start.8 = (f32[112]{0:T(128)S(1)}, f32[112]{0:T(128)}, u32[]{:S(2)}) copy-start(f32[112]{0:T(128)} %param.18) | copy-start | bytes 1348
  1.3 0.7 %copy-start.9 = (f32[112]{0:T(128)S(1)}, f32[112]{0:T(128)}, u32[]{:S(2)}) copy-start(f32[112]{0:T(128)} %param.17) | copy-start | bytes 1348
  2.0 1.2 %copy-start = (f32[16,64,256]{2,1,0:T(8,128)S(1)}, f32[16,64,256]{2,1,0:T(8,128)}, u32[]{:S(2)}) copy-start(f32[16,64,256]{2,1,0:T(8,128)} %board_hbm.1) | copy-start | bytes 3145732
  3.2 1.2 %copy-start.1 = (f32[16,64,256]{2,1,0:T(8,128)S(1)}, f32[16,64,256]{2,1,0:T(8,128)}, u32[]{:S(2)}) copy-start(f32[16,64,256]{2,1,0:T(8,128)} %coeff_hbm.1) | copy-start | bytes 3145732
  4.5 1.2 %copy-start.2 = (f32[16,64,256]{2,1,0:T(8,128)S(1)}, f32[16,64,256]{2,1,0:T(8,128)}, u32[]{:S(2)}) copy-start(f32[16,64,256]{2,1,0:T(8,128)} %target_hbm.1) | copy-start | bytes 3145732
  5.7 0.9 %copy-start.3 = (f32[112,512]{1,0:T(8,128)S(1)}, f32[112,512]{1,0:T(8,128)}, u32[]{:S(2)}) copy-start(f32[112,512]{1,0:T(8,128)} %pipe_temp_hbm.1) | copy-start | bytes 688132
  6.6 0.9 %copy-start.4 = (f32[112,512]{1,0:T(8,128)S(1)}, f32[112,512]{1,0:T(8,128)}, u32[]{:S(2)}) copy-start(f32[112,512]{1,0:T(8,128)} %pipe_target_hbm.1) | copy-start | bytes 688132
  7.6 0.9 %copy-start.5 = (s32[112,512]{1,0:T(8,128)S(1)}, s32[112,512]{1,0:T(8,128)}, u32[]{:S(2)}) copy-start(s32[112,512]{1,0:T(8,128)} %contact_hbm.1) | copy-start | bytes 688132
  8.5 0.8 %copy-start.6 = (f32[64,256]{1,0:T(8,128)S(1)}, f32[64,256]{1,0:T(8,128)}, u32[]{:S(2)}) copy-start(f32[64,256]{1,0:T(8,128)} %source_hbm.1) | copy-start | bytes 196612
